TPU v7x, 32 devices: a whole 2x2x4 slice. The times are simulated.
32 devices in a mesh: space: 4 (over y, x), spin: 2 (over core), cons: 4 (over z).
Axes of the slice: x: 2, y: 2, z: 4, core: 2. Of those that a mesh axis runs over, the one named last changes fastest.
Arguments:
- eigvecs: bfloat16 [2, 2, 256, 7680], P(None, None, None, 'space'), may hold values from -0.0625 to 0.0625
- solutions: bfloat16 [2, 2, 4, 256, 7680], P(None, None, 'spin', 'cons', 'space'), may hold values from -6 to 6
- elementals: bfloat16 [8, 2, 256, 256], replicated, may hold values from -0.375 to 0.375
- op_list: int32 [32, 16, 4], P(('space', 'spin', 'cons')), may hold values from 0 to 7, as said below
- live_count: int32 [32], P(('space', 'spin', 'cons')), may hold values from 1 to 16, as said below
Outputs:
- blocks: bfloat16 [2, 512, 256, 256], P(None, ('space', 'spin', 'cons'))
Inputs may be any that keep to these rules, and one draw needn't show every extreme that they name: `op_list`: columns hold an elemental in 0 to 7, two sink spins in 0 to 3 and a sink slice in 0 to 1; slots at or beyond an owner's live count hold arbitrary entries of that kind. `live_count`: some owner has all 16 slots live.
All inputs are finite; a program needn't handle non-finite values.
Results may differ from a plain program's by a relative error of at most 0.0064.
Values may be sent and summed in bfloat16 or wider, within the bound.
No kernel may reach another device: no remote copies, remote signals or barrier semaphores. Data moves between devices by JAX's collectives and lax.ppermute only.
A program may use at most 128 MiB of HBM per device.

v0:
```python
import functools
import math

import jax
import jax.numpy as jnp
from jax import lax
from jax.experimental import pallas as pl
from jax.experimental.pallas import tpu as pltpu
from jax.sharding import PartitionSpec as P

NT_DOT = (((1,), (1,)), ((), ()))
NN_DOT = (((1,), (0,)), ((), ()))


dot = functools.partial(lax.dot_general, preferred_element_type=jnp.float32)


def partners(n):
    if n & (n - 1) == 0:
        return [[(i, i ^ s) for i in range(n)] for s in range(n)]
    return [[(i, (i + s) % n) for i in range(n)] for s in range(n)]


def partner(index, step, n):
    if n & (n - 1) == 0:
        return index ^ step
    return lax.rem(index - step + n, n)


def target(index, step, n):
    if n & (n - 1) == 0:
        return index ^ step
    return lax.rem(index + step, n)


def depth_cuts(depth):
    half = max(256, (depth // 2 + 255) // 256 * 256)
    return [(0, half), (half, depth)] if half < depth else [(0, depth)]


def partial_kernel(n_space, cuts, v_ref, s_ref, *rest):
    outs = rest[:n_space]
    v_buf, s_buf, acc, in_sem = rest[n_space:]
    _, nt, nev, _ = v_ref.shape
    _, _, nsp, nj, _ = s_ref.shape
    copies = []
    for t in range(nt):
        for c, (lo, hi) in enumerate(cuts):
            group = []
            for p in range(2):
                group += [
                    pltpu.make_async_copy(
                        v_ref.at[p, t, :, lo:hi], v_buf.at[p, t, :, lo:hi], in_sem.at[t, c, 2 * p]
                    ),
                    pltpu.make_async_copy(
                        s_ref.at[p, t, :, :, lo:hi],
                        s_buf.at[p, t, :, :, lo:hi],
                        in_sem.at[t, c, 2 * p + 1],
                    ),
                ]
            for copy in group:
                copy.start()
            copies.append(group)
    for t in range(nt):
        total = None
        for c, (lo, hi) in enumerate(cuts):
            for copy in copies[t * len(cuts) + c]:
                copy.wait()
            vr, vi = v_buf[0, t, :, lo:hi], v_buf[1, t, :, lo:hi]
            sr = s_buf[0, t, :, :, lo:hi].reshape(nsp * nj, hi - lo)
            si = s_buf[1, t, :, :, lo:hi].reshape(nsp * nj, hi - lo)
            both = dot(jnp.concatenate([sr, si]), vr, NT_DOT) + dot(
                jnp.concatenate([si, -sr]), vi, NT_DOT
            )
            total = both if total is None else total + both
        total = total.reshape(2, nsp, nj, nev)
        for sp in range(nsp):
            for p in range(2):
                start = ((t * nsp + sp) * 2 + p) * nj
                acc[start : start + nj, :] = total[p, sp]
    chunk = acc.shape[0] // n_space
    me = lax.axis_index("space")
    for s in range(n_space):
        first = pl.multiple_of(target(me, s, n_space) * chunk, chunk)
        outs[s][...] = acc[pl.ds(first, chunk), :].astype(outs[s].dtype)


def partial_taus(eigvecs, solutions, n_space, send_type):
    _, nt, nev, depth = eigvecs.shape
    _, _, nsp, nj, _ = solutions.shape
    rows = nt * nsp * 2 * nj
    cuts = depth_cuts(depth)
    chunk = (rows // n_space, nev)
    return pl.pallas_call(
        functools.partial(partial_kernel, n_space, cuts),
        out_shape=[pltpu.VMEM(chunk, jnp.float32)] + [pltpu.VMEM(chunk, send_type)] * (n_space - 1),
        in_specs=[pl.BlockSpec(memory_space=pl.ANY)] * 2,
        out_specs=[pl.BlockSpec(memory_space=pltpu.VMEM)] * n_space,
        scratch_shapes=[
            pltpu.VMEM(eigvecs.shape, eigvecs.dtype),
            pltpu.VMEM(solutions.shape, solutions.dtype),
            pltpu.VMEM((rows, nev), jnp.float32),
            pltpu.SemaphoreType.DMA((nt, len(cuts), 4)),
        ],
        compiler_params=pltpu.CompilerParams(vmem_limit_bytes=32 * 2**20),
        cost_estimate=pl.CostEstimate(
            flops=4 * rows * nev * depth,
            bytes_accessed=2 * (eigvecs.size + solutions.size) + 4 * rows * nev,
            transcendentals=0,
        ),
    )(
        pltpu.with_memory_space_constraint(eigvecs, pltpu.HBM),
        pltpu.with_memory_space_constraint(solutions, pltpu.HBM),
    )


def contract_kernel(layout, per_chunk, group, item_ref, live_ref, elems, *rest):
    n_space, n_spin, n_cons, nt, nsp, nj = layout
    n_parts = n_space * n_spin
    parts, out_ref = rest[:n_parts], rest[n_parts]
    tau, outs, mid, tau_sem, out_sem = rest[n_parts + 1 :]
    unit, nev = tau.shape[-2:]
    slots = out_ref.shape[1]
    scale = nev ** (-0.5)
    space, spin, cons = (lax.axis_index(a) for a in ("space", "spin", "cons"))
    loads = [pltpu.make_async_copy(part, tau.at[n], tau_sem.at[n]) for n, part in enumerate(parts)]
    for copy in loads:
        copy.start()
    for copy in loads:
        copy.wait()

    def matrix(t, a, p):
        first = ((t * nsp + a % nsp) * 2 + p) * (nj // unit)
        rows = []
        for z in range(n_cons):
            z_step = step_from(z, cons, n_cons)
            for k in range(nj // unit):
                where = first + k
                part = step_from(a // nsp, spin, n_spin) * n_space + step_from(
                    where // per_chunk, space, n_space
                )
                rows.append(tau[part, z_step * per_chunk + where % per_chunk])
        return jnp.concatenate(rows)

    def write(k):
        return pltpu.make_async_copy(outs.at[k], out_ref.at[:, k], out_sem.at[k])

    def right_half(u, item):
        e, _, b, t = item
        er, ei = elems[e, 0], elems[e, 1]
        tau_b = jnp.concatenate([matrix(t, b, 0), matrix(t, b, 1)], axis=1)
        real = dot(jnp.concatenate([er, -ei], axis=1), tau_b, NT_DOT)
        imag = dot(jnp.concatenate([ei, er], axis=1), tau_b, NT_DOT)
        mid[u, :nev] = real.astype(mid.dtype)
        mid[u, nev:] = imag.astype(mid.dtype)

    def left_half(u, k, item):
        _, a, _, t = item
        ar, ai = matrix(t, a, 0), matrix(t, a, 1)
        keep = k < live_ref[0]
        real = dot(jnp.concatenate([ar, ai], axis=1), mid[u], NN_DOT)
        imag = dot(jnp.concatenate([-ai, ar], axis=1), mid[u], NN_DOT)
        outs[k, 0] = jnp.where(keep, real * scale, 0.0).astype(outs.dtype)
        outs[k, 1] = jnp.where(keep, imag * scale, 0.0).astype(outs.dtype)

    def one_group(g, carry):
        ks = [g * group + u for u in range(group)]
        items = [tuple(item_ref[4 * k + n] for n in range(4)) for k in ks]
        right_half(0, items[0])
        for u in range(group):
            if u + 1 < group:
                right_half(u + 1, items[u + 1])
            left_half(u, ks[u], items[u])
        for k in ks:
            write(k).start()
        return carry

    def empty_group(g, carry):
        for u in range(group):
            k = g * group + u
            outs[k] = jnp.zeros(outs.shape[1:], outs.dtype)
            write(k).start()
        return carry

    n_groups = slots // group
    used = lax.div(live_ref[0] + group - 1, group)
    lax.fori_loop(0, used, one_group, 0)
    lax.fori_loop(used, n_groups, empty_group, 0)
    for k in range(slots):
        write(k).wait()


def step_from(sender, me, n):
    if n & (n - 1) == 0:
        return sender ^ me
    return lax.rem(me - sender + n, n)


def contract(items, live, elementals, parts, layout):
    n_space, n_spin, n_cons, nt, nsp, nj = layout
    slots = items.shape[0]
    nev = elementals.shape[-1]
    chunk = parts[0].shape[-2]
    unit = min(chunk, nj)
    group = math.gcd(slots, 4)
    parts = [part.reshape(n_cons * chunk // unit, unit, nev) for part in parts]
    return pl.pallas_call(
        functools.partial(contract_kernel, layout, chunk // unit, group),
        out_shape=jax.ShapeDtypeStruct((2, slots, nev, nev), jnp.bfloat16),
        in_specs=[pl.BlockSpec(memory_space=pltpu.SMEM)] * 2
        + [pl.BlockSpec(memory_space=pltpu.VMEM)] * (1 + len(parts)),
        out_specs=pl.BlockSpec(memory_space=pl.ANY),
        scratch_shapes=[
            pltpu.VMEM((len(parts),) + parts[0].shape, jnp.bfloat16),
            pltpu.VMEM((slots, 2, nev, nev), jnp.bfloat16),
            pltpu.VMEM((group, 2 * nev, nev), jnp.bfloat16),
            pltpu.SemaphoreType.DMA((len(parts),)),
            pltpu.SemaphoreType.DMA((slots,)),
        ],
        compiler_params=pltpu.CompilerParams(vmem_limit_bytes=32 * 2**20),
        cost_estimate=pl.CostEstimate(
            flops=16 * slots * nev**3,
            bytes_accessed=2 * (elementals.size + 2 * slots * nev * nev),
            transcendentals=0,
        ),
    )(
        items.reshape(-1),
        live,
        *(pltpu.with_memory_space_constraint(x, pltpu.VMEM) for x in [elementals] + parts),
    )


def body(eigvecs, solutions, elementals, op_list, live_count):
    n_space, n_spin, n_cons = (lax.axis_size(a) for a in ("space", "spin", "cons"))
    _, nt, nsp, nj, _ = solutions.shape
    sends = partial_taus(eigvecs, solutions, n_space, jnp.bfloat16)
    elementals, sends = lax.optimization_barrier((elementals, sends))
    space_steps, spin_steps, cons_steps = partners(n_space), partners(n_spin), partners(n_cons)
    got = [sends[0]] + [
        lax.ppermute(sends[s], "space", space_steps[s]) for s in range(1, n_space)
    ]
    mine = functools.reduce(jnp.add, [part.astype(jnp.float32) for part in got]).astype(jnp.bfloat16)
    column = jnp.stack(
        [mine] + [lax.ppermute(mine, "cons", cons_steps[s]) for s in range(1, n_cons)]
    )
    plane = [column] + [
        lax.ppermute(column, "space", space_steps[s]) for s in range(1, n_space)
    ]
    parts = list(plane)
    for s in range(1, n_spin):
        parts += [lax.ppermute(part, "spin", spin_steps[s]) for part in plane]
    layout = (n_space, n_spin, n_cons, nt, nsp, nj)
    return contract(op_list[0], live_count, elementals, parts, layout)


def solution(mesh):
    return jax.shard_map(
        body,
        mesh=mesh,
        in_specs=(
            P(None, None, None, "space"),
            P(None, None, "spin", "cons", "space"),
            P(),
            P(("space", "spin", "cons"), None, None),
            P(("space", "spin", "cons")),
        ),
        out_specs=P(None, ("space", "spin", "cons"), None, None),
        check_vma=False,
    )
```

profile of v0, /device:TPU:0, one launch (start us, length us, event | category | flops | bytes accessed | tf_op | source)
XLA Modules:
  0.0 45.3 jit_solution(6228953376541761328)
XLA Ops:
  0.0 0.0 copy-start
  0.0 0.0 copy-start.1
  0.0 4.4 %shard_map.55 = (f32[128,256]{1,0:T(8,128)S(1)}, bf16[128,256]{1,0:T(8,128)(2,1)S(1)}, bf16[128,256]{1,0:T(8,128)(2,1)S(1)}, bf16[128,256]{1,0:T(8,128)(2,1)S(1)}) custom-call(bf16[2,2,256,1920]{3,2,1,0:T(8,128)(2,1)} %v_ref.1, bf16[2,2,2,64,1920]{4,3,2,1,0:T(8,128)(2,1)} %s_ref.1), custom_call_target="tpu_custom_call" | custom-call | flops 1006632960 | bytes 6422528 | tf_op jit(solution)/shard_map/pallas_call | solution.py:94
  4.4 3.0 %collective-permute-start = (bf16[128,256]{1,0:T(8,128)(2,1)S(1)}, bf16[128,256]{1,0:T(8,128)(2,1)S(1)}, u32[]{:S(2)}, u32[]{:S(2)}) collective-permute-start(bf16[128,256]{1,0:T(8,128)(2,1)S(1)} %get-tuple-element.20), channel_id=1, source_target_pairs={{0,8},{8,0},{16,24},{24,16},{1,9},{9,1},{17,25},{25,17},{2,10},{10... | collective-permute-start | bytes 196616 | tf_op jit(solution)/shard_map/ppermute | solution.py:240
  7.4 1.5 %collective-permute-start.1 = (bf16[128,256]{1,0:T(8,128)(2,1)S(1)}, bf16[128,256]{1,0:T(8,128)(2,1)S(1)}, u32[]{:S(2)}, u32[]{:S(2)}) collective-permute-start(bf16[128,256]{1,0:T(8,128)(2,1)S(1)} %get-tuple-element.21), channel_id=1, source_target_pairs={{0,16},{8,24},{16,0},{24,8},{1,17},{9,25},{17,1},{25,9},{2,18},{10... | collective-permute-start | bytes 196616 | tf_op jit(solution)/shard_map/ppermute | solution.py:240
  8.9 0.0 collective-permute-start.2
  8.9 0.8 %collective-permute-done = bf16[128,256]{1,0:T(8,128)(2,1)S(1)} collective-permute-done((bf16[128,256]{1,0:T(8,128)(2,1)S(1)}, bf16[128,256]{1,0:T(8,128)(2,1)S(1)}, u32[]{:S(2)}, u32[]{:S(2)}) %collective-permute-start) | collective-permute-done | bytes 65568 | tf_op jit(solution)/shard_map/ppermute | solution.py:240
  9.7 1.9 %collective-permute-done.1 = bf16[128,256]{1,0:T(8,128)(2,1)S(1)} collective-permute-done((bf16[128,256]{1,0:T(8,128)(2,1)S(1)}, bf16[128,256]{1,0:T(8,128)(2,1)S(1)}, u32[]{:S(2)}, u32[]{:S(2)}) %collective-permute-start.1) | collective-permute-done | bytes 65568 | tf_op jit(solution)/shard_map/ppermute | solution.py:240
  11.6 2.4 %collective-permute-done.2 = bf16[128,256]{1,0:T(8,128)(2,1)S(1)} collective-permute-done((bf16[128,256]{1,0:T(8,128)(2,1)S(1)}, bf16[128,256]{1,0:T(8,128)(2,1)S(1)}, u32[]{:S(2)}, u32[]{:S(2)}) %collective-permute-start.2) | collective-permute-done | bytes 65568 | tf_op jit(solution)/shard_map/ppermute | solution.py:240
  14.1 3.7 %collective-permute-start.5 = (bf16[128,256]{1,0:T(8,128)(2,1)S(1)}, bf16[128,256]{1,0:T(8,128)(2,1)S(1)}, u32[]{:S(2)}, u32[]{:S(2)}) collective-permute-start(bf16[128,256]{1,0:T(8,128)(2,1)S(1)} %add_convert_fusion), channel_id=1, source_target_pairs={{0,3},{1,2},{2,1},{3,0},{4,7},{5,6},{6,5},{7,4},{8,11},{9,10},{10,... | collective-permute-start | bytes 196616 | tf_op jit(solution)/shard_map/ppermute | solution.py:244
  17.8 0.0 collective-permute-start.4
  17.8 0.8 %collective-permute-start.3 = (bf16[128,256]{1,0:T(8,128)(2,1)S(1)}, bf16[128,256]{1,0:T(8,128)(2,1)S(1)}, u32[]{:S(2)}, u32[]{:S(2)}) collective-permute-start(bf16[128,256]{1,0:T(8,128)(2,1)S(1)} %add_convert_fusion), channel_id=1, source_target_pairs={{0,1},{1,0},{2,3},{3,2},{4,5},{5,4},{6,7},{7,6},{8,9},{9,8},{10,11... | collective-permute-start | bytes 196616 | tf_op jit(solution)/shard_map/ppermute | solution.py:244
  18.6 1.8 %collective-permute-done.5 = bf16[128,256]{1,0:T(8,128)(2,1)S(1)} collective-permute-done((bf16[128,256]{1,0:T(8,128)(2,1)S(1)}, bf16[128,256]{1,0:T(8,128)(2,1)S(1)}, u32[]{:S(2)}, u32[]{:S(2)}) %collective-permute-start.5) | collective-permute-done | bytes 65568 | tf_op jit(solution)/shard_map/ppermute | solution.py:244
  20.3 2.6 %collective-permute-done.4 = bf16[128,256]{1,0:T(8,128)(2,1)S(1)} collective-permute-done((bf16[128,256]{1,0:T(8,128)(2,1)S(1)}, bf16[128,256]{1,0:T(8,128)(2,1)S(1)}, u32[]{:S(2)}, u32[]{:S(2)}) %collective-permute-start.4) | collective-permute-done | bytes 65568 | tf_op jit(solution)/shard_map/ppermute | solution.py:244
  22.9 0.0 collective-permute-done.3
  23.0 0.5 %collective-permute-start.8 = (bf16[4,128,256]{2,1,0:T(8,128)(2,1)S(1)}, bf16[4,128,256]{2,1,0:T(8,128)(2,1)S(1)}, u32[]{:S(2)}, u32[]{:S(2)}) collective-permute-start(bf16[4,128,256]{2,1,0:T(8,128)(2,1)S(1)} %pad_maximum_fusion), channel_id=1, source_target_pairs={{0,24},{8,16},{16,8},{24,0},{1,25},{9,17},{17,9},{25,1},{2,26},{10... | collective-permute-start | bytes 786440 | tf_op jit(solution)/shard_map/ppermute | solution.py:247
  23.5 1.5 %collective-permute-start.7 = (bf16[4,128,256]{2,1,0:T(8,128)(2,1)S(1)}, bf16[4,128,256]{2,1,0:T(8,128)(2,1)S(1)}, u32[]{:S(2)}, u32[]{:S(2)}) collective-permute-start(bf16[4,128,256]{2,1,0:T(8,128)(2,1)S(1)} %pad_maximum_fusion), channel_id=1, source_target_pairs={{0,16},{8,24},{16,0},{24,8},{1,17},{9,25},{17,1},{25,9},{2,18},{10... | collective-permute-start | bytes 786440 | tf_op jit(solution)/shard_map/ppermute | solution.py:247
  25.0 1.5 %collective-permute-start.6 = (bf16[4,128,256]{2,1,0:T(8,128)(2,1)S(1)}, bf16[4,128,256]{2,1,0:T(8,128)(2,1)S(1)}, u32[]{:S(2)}, u32[]{:S(2)}) collective-permute-start(bf16[4,128,256]{2,1,0:T(8,128)(2,1)S(1)} %pad_maximum_fusion), channel_id=1, source_target_pairs={{0,8},{8,0},{16,24},{24,16},{1,9},{9,1},{17,25},{25,17},{2,10},{10... | collective-permute-start | bytes 786440 | tf_op jit(solution)/shard_map/ppermute | solution.py:247
  26.5 0.0 collective-permute-start.9
  26.5 6.3 %collective-permute-done.8 = bf16[4,128,256]{2,1,0:T(8,128)(2,1)S(1)} collective-permute-done((bf16[4,128,256]{2,1,0:T(8,128)(2,1)S(1)}, bf16[4,128,256]{2,1,0:T(8,128)(2,1)S(1)}, u32[]{:S(2)}, u32[]{:S(2)}) %collective-permute-start.8) | collective-permute-done | bytes 262176 | tf_op jit(solution)/shard_map/ppermute | solution.py:247
  32.8 0.0 collective-permute-start.12
  32.8 2.7 %collective-permute-done.7 = bf16[4,128,256]{2,1,0:T(8,128)(2,1)S(1)} collective-permute-done((bf16[4,128,256]{2,1,0:T(8,128)(2,1)S(1)}, bf16[4,128,256]{2,1,0:T(8,128)(2,1)S(1)}, u32[]{:S(2)}, u32[]{:S(2)}) %collective-permute-start.7) | collective-permute-done | bytes 262176 | tf_op jit(solution)/shard_map/ppermute | solution.py:247
  35.6 0.0 collective-permute-start.11
  35.6 0.0 collective-permute-done.6
  35.6 0.5 %collective-permute-start.10 = (bf16[4,128,256]{2,1,0:T(8,128)(2,1)S(1)}, bf16[4,128,256]{2,1,0:T(8,128)(2,1)}, u32[]{:S(2)}, u32[]{:S(2)}) collective-permute-start(bf16[4,128,256]{2,1,0:T(8,128)(2,1)S(1)} %collective-permute-done.6), channel_id=1, source_target_pairs={{0,4},{4,0},{1,5},{5,1},{2,6},{6,2},{3,7},{7,3},{8,12},{12,8},{9,1... | collective-permute-start | bytes 786440 | tf_op jit(solution)/shard_map/ppermute | solution.py:251
  36.7 0.0 copy-done.1
  36.7 0.1 copy.7
  36.8 0.1 reshape_squeeze.3.item_ref
  36.9 0.0 collective-permute-done.9
  36.9 0.0 collective-permute-done.12
  36.9 0.3 collective-permute-done.11
  37.2 0.4 collective-permute-done.10
  37.6 0.0 copy-done
  37.6 7.7 %shard_map.56 = bf16[2,16,256,256]{3,2,1,0:T(8,128)(2,1)} custom-call(s32[64]{0:T(128)S(1)} %reshape_squeeze.3.item_ref, s32[1]{0:T(128)S(6)} %copy.8.live_ref, bf16[8,2,256,256]{3,2,1,0:T(8,128)(2,1)S(1)} %copy-done, bf16[8,64,256]{2,1,0:T(8,128)(2,1)S(1)} %bitcast.12, bf16[8,64,256]{2,1,0:T(8,128)(2,1)S(1)} %bitcast.15, bf16[8,64,256]{2,1,0:T(8,128)(2,1)S(1)} %bitcast.14, ...), custom_call_target="tpu_custom_call" | custom-call | flops 4294967296 | bytes 6291456 | tf_op jit(solution)/shard_map/pallas_call | solution.py:207
  (2 shorter events, 0.1 us)
Async XLA Ops:
  0.0 37.6 %copy-start = (bf16[8,2,256,256]{3,2,1,0:T(8,128)(2,1)S(1)}, bf16[8,2,256,256]{3,2,1,0:T(8,128)(2,1)}, u32[]{:S(2)}) copy-start(bf16[8,2,256,256]{3,2,1,0:T(8,128)(2,1)} %elems) | copy-start | bytes 6291460
  0.0 36.7 %copy-start.1 = (s32[1,16,4]{1,2,0:T(4,128)S(1)}, s32[1,16,4]{1,2,0:T(4,128)}, u32[]{:S(2)}) copy-start(s32[1,16,4]{1,2,0:T(4,128)} %param.8) | copy-start | bytes 772
  4.4 5.4 %collective-permute-start = (bf16[128,256]{1,0:T(8,128)(2,1)S(1)}, bf16[128,256]{1,0:T(8,128)(2,1)S(1)}, u32[]{:S(2)}, u32[]{:S(2)}) collective-permute-start(bf16[128,256]{1,0:T(8,128)(2,1)S(1)} %get-tuple-element.20), channel_id=1, source_target_pairs={{0,8},{8,0},{16,24},{24,16},{1,9},{9,1},{17,25},{25,17},{2,10},{10... | collective-permute-start | bytes 196616 | tf_op jit(solution)/shard_map/ppermute | solution.py:240
  7.4 4.3 %collective-permute-start.1 = (bf16[128,256]{1,0:T(8,128)(2,1)S(1)}, bf16[128,256]{1,0:T(8,128)(2,1)S(1)}, u32[]{:S(2)}, u32[]{:S(2)}) collective-permute-start(bf16[128,256]{1,0:T(8,128)(2,1)S(1)} %get-tuple-element.21), channel_id=1, source_target_pairs={{0,16},{8,24},{16,0},{24,8},{1,17},{9,25},{17,1},{25,9},{2,18},{10... | collective-permute-start | bytes 196616 | tf_op jit(solution)/shard_map/ppermute | solution.py:240
  8.9 5.2 %collective-permute-start.2 = (bf16[128,256]{1,0:T(8,128)(2,1)S(1)}, bf16[128,256]{1,0:T(8,128)(2,1)S(1)}, u32[]{:S(2)}, u32[]{:S(2)}) collective-permute-start(bf16[128,256]{1,0:T(8,128)(2,1)S(1)} %get-tuple-element.22), channel_id=1, source_target_pairs={{0,24},{8,16},{16,8},{24,0},{1,25},{9,17},{17,9},{25,1},{2,26},{10... | collective-permute-start | bytes 196616 | tf_op jit(solution)/shard_map/ppermute | solution.py:240
  14.1 6.2 %collective-permute-start.5 = (bf16[128,256]{1,0:T(8,128)(2,1)S(1)}, bf16[128,256]{1,0:T(8,128)(2,1)S(1)}, u32[]{:S(2)}, u32[]{:S(2)}) collective-permute-start(bf16[128,256]{1,0:T(8,128)(2,1)S(1)} %add_convert_fusion), channel_id=1, source_target_pairs={{0,3},{1,2},{2,1},{3,0},{4,7},{5,6},{6,5},{7,4},{8,11},{9,10},{10,... | collective-permute-start | bytes 196616 | tf_op jit(solution)/shard_map/ppermute | solution.py:244
  17.8 5.2 %collective-permute-start.4 = (bf16[128,256]{1,0:T(8,128)(2,1)S(1)}, bf16[128,256]{1,0:T(8,128)(2,1)S(1)}, u32[]{:S(2)}, u32[]{:S(2)}) collective-permute-start(bf16[128,256]{1,0:T(8,128)(2,1)S(1)} %add_convert_fusion), channel_id=1, source_target_pairs={{0,2},{1,3},{2,0},{3,1},{4,6},{5,7},{6,4},{7,5},{8,10},{9,11},{10,... | collective-permute-start | bytes 196616 | tf_op jit(solution)/shard_map/ppermute | solution.py:244
  17.8 5.2 %collective-permute-start.3 = (bf16[128,256]{1,0:T(8,128)(2,1)S(1)}, bf16[128,256]{1,0:T(8,128)(2,1)S(1)}, u32[]{:S(2)}, u32[]{:S(2)}) collective-permute-start(bf16[128,256]{1,0:T(8,128)(2,1)S(1)} %add_convert_fusion), channel_id=1, source_target_pairs={{0,1},{1,0},{2,3},{3,2},{4,5},{5,4},{6,7},{7,6},{8,9},{9,8},{10,11... | collective-permute-start | bytes 196616 | tf_op jit(solution)/shard_map/ppermute | solution.py:244
  23.0 9.9 %collective-permute-start.8 = (bf16[4,128,256]{2,1,0:T(8,128)(2,1)S(1)}, bf16[4,128,256]{2,1,0:T(8,128)(2,1)S(1)}, u32[]{:S(2)}, u32[]{:S(2)}) collective-permute-start(bf16[4,128,256]{2,1,0:T(8,128)(2,1)S(1)} %pad_maximum_fusion), channel_id=1, source_target_pairs={{0,24},{8,16},{16,8},{24,0},{1,25},{9,17},{17,9},{25,1},{2,26},{10... | collective-permute-start | bytes 786440 | tf_op jit(solution)/shard_map/ppermute | solution.py:247
  23.5 12.1 %collective-permute-start.7 = (bf16[4,128,256]{2,1,0:T(8,128)(2,1)S(1)}, bf16[4,128,256]{2,1,0:T(8,128)(2,1)S(1)}, u32[]{:S(2)}, u32[]{:S(2)}) collective-permute-start(bf16[4,128,256]{2,1,0:T(8,128)(2,1)S(1)} %pad_maximum_fusion), channel_id=1, source_target_pairs={{0,16},{8,24},{16,0},{24,8},{1,17},{9,25},{17,1},{25,9},{2,18},{10... | collective-permute-start | bytes 786440 | tf_op jit(solution)/shard_map/ppermute | solution.py:247
  25.0 10.6 %collective-permute-start.6 = (bf16[4,128,256]{2,1,0:T(8,128)(2,1)S(1)}, bf16[4,128,256]{2,1,0:T(8,128)(2,1)S(1)}, u32[]{:S(2)}, u32[]{:S(2)}) collective-permute-start(bf16[4,128,256]{2,1,0:T(8,128)(2,1)S(1)} %pad_maximum_fusion), channel_id=1, source_target_pairs={{0,8},{8,0},{16,24},{24,16},{1,9},{9,1},{17,25},{25,17},{2,10},{10... | collective-permute-start | bytes 786440 | tf_op jit(solution)/shard_map/ppermute | solution.py:247
  26.5 10.4 %collective-permute-start.9 = (bf16[4,128,256]{2,1,0:T(8,128)(2,1)S(1)}, bf16[4,128,256]{2,1,0:T(8,128)(2,1)S(1)}, u32[]{:S(2)}, u32[]{:S(2)}) collective-permute-start(bf16[4,128,256]{2,1,0:T(8,128)(2,1)S(1)} %pad_maximum_fusion), channel_id=1, source_target_pairs={{0,4},{4,0},{1,5},{5,1},{2,6},{6,2},{3,7},{7,3},{8,12},{12,8},{9,1... | collective-permute-start | bytes 786440 | tf_op jit(solution)/shard_map/ppermute | solution.py:251
  32.8 4.1 %collective-permute-start.12 = (bf16[4,128,256]{2,1,0:T(8,128)(2,1)S(1)}, bf16[4,128,256]{2,1,0:T(8,128)(2,1)}, u32[]{:S(2)}, u32[]{:S(2)}) collective-permute-start(bf16[4,128,256]{2,1,0:T(8,128)(2,1)S(1)} %collective-permute-done.8), channel_id=1, source_target_pairs={{0,4},{4,0},{1,5},{5,1},{2,6},{6,2},{3,7},{7,3},{8,12},{12,8},{9,1... | collective-permute-start | bytes 786440 | tf_op jit(solution)/shard_map/ppermute | solution.py:251
  35.6 1.7 %collective-permute-start.11 = (bf16[4,128,256]{2,1,0:T(8,128)(2,1)S(1)}, bf16[4,128,256]{2,1,0:T(8,128)(2,1)}, u32[]{:S(2)}, u32[]{:S(2)}) collective-permute-start(bf16[4,128,256]{2,1,0:T(8,128)(2,1)S(1)} %collective-permute-done.7), channel_id=1, source_target_pairs={{0,4},{4,0},{1,5},{5,1},{2,6},{6,2},{3,7},{7,3},{8,12},{12,8},{9,1... | collective-permute-start | bytes 786440 | tf_op jit(solution)/shard_map/ppermute | solution.py:251
  35.6 2.0 %collective-permute-start.10 = (bf16[4,128,256]{2,1,0:T(8,128)(2,1)S(1)}, bf16[4,128,256]{2,1,0:T(8,128)(2,1)}, u32[]{:S(2)}, u32[]{:S(2)}) collective-permute-start(bf16[4,128,256]{2,1,0:T(8,128)(2,1)S(1)} %collective-permute-done.6), channel_id=1, source_target_pairs={{0,4},{4,0},{1,5},{5,1},{2,6},{6,2},{3,7},{7,3},{8,12},{12,8},{9,1... | collective-permute-start | bytes 786440 | tf_op jit(solution)/shard_map/ppermute | solution.py:251
where the time goes:
time: 45.3 us
  waiting for transfers between devices  19.2 us (42%)
  starting transfers between devices  13.1 us (29%)
  Pallas kernels  12.1 us (27%)
  between operations  0.71 us (2%)
    ppermute x3, waiting for transfers between devices, body(): lax.ppermute(column, 'space', space_steps[s])  9.02 us
    pallas_call x1, Pallas kernels, contract(): pl.pallas_call(functools.partial(contract_kernel, layout, chunk // unit,...  7.73 us
    ppermute x3, waiting for transfers between devices, body(): lax.ppermute(sends[s], 'space', space_steps[s])  5.16 us
    ppermute x3, starting transfers between devices, body(): lax.ppermute(sends[s], 'space', space_steps[s])  4.54 us
    ppermute x3, starting transfers between devices, body(): lax.ppermute(mine, 'cons', cons_steps[s])  4.45 us
    ppermute x3, waiting for transfers between devices, body(): lax.ppermute(mine, 'cons', cons_steps[s])  4.38 us
    pallas_call x1, Pallas kernels, partial_taus(): pl.pallas_call(functools.partial(partial_kernel, n_space, cuts), out_shap...  4.36 us
    ppermute x3, starting transfers between devices, body(): lax.ppermute(column, 'space', space_steps[s])  3.55 us
  transfers between devices with their start and end apart: 13, of which 9 were waited for; matrix products, arithmetic and copies ran while one was open for 0% of the time, Pallas kernels for 0%

commit v1 on v0

--- a/solution.py
+++ b/solution.py
@@ -81,8 +81,8 @@
     chunk = acc.shape[0] // n_space
     me = lax.axis_index("space")
     for s in range(n_space):
-        first = pl.multiple_of(target(me, s, n_space) * chunk, chunk)
-        outs[s][...] = acc[pl.ds(first, chunk), :].astype(outs[s].dtype)
+        rows = pl.ds(pl.multiple_of(target(me, s, n_space) * chunk, chunk), chunk)
+        outs[s][...] = acc[rows, :].astype(outs[s].dtype)
 
 
 def partial_taus(eigvecs, solutions, n_space, send_type):
@@ -114,18 +114,23 @@
     )
 
 
-def contract_kernel(layout, per_chunk, group, item_ref, live_ref, elems, *rest):
+def contract_kernel(layout, firsts, per_chunk, group, item_in, live_in, elems, *rest):
     n_space, n_spin, n_cons, nt, nsp, nj = layout
-    n_parts = n_space * n_spin
+    n_parts = len(firsts)
     parts, out_ref = rest[:n_parts], rest[n_parts]
-    tau, outs, mid, tau_sem, out_sem = rest[n_parts + 1 :]
+    tau, outs, mid, item_ref, live_ref, out_sem, slot_sem = rest[n_parts + 1 :]
     unit, nev = tau.shape[-2:]
     slots = out_ref.shape[1]
     scale = nev ** (-0.5)
     space, spin, cons = (lax.axis_index(a) for a in ("space", "spin", "cons"))
-    loads = [pltpu.make_async_copy(part, tau.at[n], tau_sem.at[n]) for n, part in enumerate(parts)]
+    loads = [
+        pltpu.make_async_copy(item_in, item_ref, slot_sem.at[0]),
+        pltpu.make_async_copy(live_in, live_ref, slot_sem.at[1]),
+    ]
     for copy in loads:
         copy.start()
+    for part, first in zip(parts, firsts):
+        tau[first : first + part.shape[0]] = part[...]
     for copy in loads:
         copy.wait()
 
@@ -136,10 +141,9 @@
             z_step = step_from(z, cons, n_cons)
             for k in range(nj // unit):
                 where = first + k
-                part = step_from(a // nsp, spin, n_spin) * n_space + step_from(
-                    where // per_chunk, space, n_space
-                )
-                rows.append(tau[part, z_step * per_chunk + where % per_chunk])
+                step = step_from(where // per_chunk, space, n_space)
+                part = step_from(a // nsp, spin, n_spin) * n_space + step
+                rows.append(tau[(part * n_cons + z_step) * per_chunk + where % per_chunk])
         return jnp.concatenate(rows)
 
     def write(k):
@@ -165,14 +169,13 @@
 
     def one_group(g, carry):
         ks = [g * group + u for u in range(group)]
-        items = [tuple(item_ref[4 * k + n] for n in range(4)) for k in ks]
+        items = [tuple(item_ref[n, k] for n in range(4)) for k in ks]
         right_half(0, items[0])
         for u in range(group):
             if u + 1 < group:
                 right_half(u + 1, items[u + 1])
             left_half(u, ks[u], items[u])
-        for k in ks:
-            write(k).start()
+            write(ks[u]).start()
         return carry
 
     def empty_group(g, carry):
@@ -196,26 +199,29 @@
     return lax.rem(me - sender + n, n)
 
 
-def contract(items, live, elementals, parts, layout):
+def contract(items, live, elementals, parts, firsts, layout):
     n_space, n_spin, n_cons, nt, nsp, nj = layout
-    slots = items.shape[0]
+    slots = items.shape[1]
     nev = elementals.shape[-1]
-    chunk = parts[0].shape[-2]
+    chunk = nt * nsp * 2 * nj // n_space
     unit = min(chunk, nj)
     group = math.gcd(slots, 4)
-    parts = [part.reshape(n_cons * chunk // unit, unit, nev) for part in parts]
+    parts = [part.reshape(-1, unit, nev) for part in parts]
+    firsts = [first // unit for first in firsts]
     return pl.pallas_call(
-        functools.partial(contract_kernel, layout, chunk // unit, group),
+        functools.partial(contract_kernel, layout, firsts, chunk // unit, group),
         out_shape=jax.ShapeDtypeStruct((2, slots, nev, nev), jnp.bfloat16),
-        in_specs=[pl.BlockSpec(memory_space=pltpu.SMEM)] * 2
+        in_specs=[pl.BlockSpec(memory_space=pl.ANY)] * 2
         + [pl.BlockSpec(memory_space=pltpu.VMEM)] * (1 + len(parts)),
         out_specs=pl.BlockSpec(memory_space=pl.ANY),
         scratch_shapes=[
-            pltpu.VMEM((len(parts),) + parts[0].shape, jnp.bfloat16),
+            pltpu.VMEM((n_space * n_spin * n_cons * chunk // unit, unit, nev), jnp.bfloat16),
             pltpu.VMEM((slots, 2, nev, nev), jnp.bfloat16),
             pltpu.VMEM((group, 2 * nev, nev), jnp.bfloat16),
-            pltpu.SemaphoreType.DMA((len(parts),)),
+            pltpu.SMEM(items.shape, jnp.int32),
+            pltpu.SMEM(live.shape, jnp.int32),
             pltpu.SemaphoreType.DMA((slots,)),
+            pltpu.SemaphoreType.DMA((2,)),
         ],
         compiler_params=pltpu.CompilerParams(vmem_limit_bytes=32 * 2**20),
         cost_estimate=pl.CostEstimate(
@@ -224,7 +230,7 @@
             transcendentals=0,
         ),
     )(
-        items.reshape(-1),
+        items,
         live,
         *(pltpu.with_memory_space_constraint(x, pltpu.VMEM) for x in [elementals] + parts),
     )
@@ -232,25 +238,42 @@
 
 def body(eigvecs, solutions, elementals, op_list, live_count):
     n_space, n_spin, n_cons = (lax.axis_size(a) for a in ("space", "spin", "cons"))
-    _, nt, nsp, nj, _ = solutions.shape
+    _, nt, nev, _ = eigvecs.shape
+    _, _, nsp, nj, _ = solutions.shape
     sends = partial_taus(eigvecs, solutions, n_space, jnp.bfloat16)
     elementals, sends = lax.optimization_barrier((elementals, sends))
     space_steps, spin_steps, cons_steps = partners(n_space), partners(n_spin), partners(n_cons)
-    got = [sends[0]] + [
-        lax.ppermute(sends[s], "space", space_steps[s]) for s in range(1, n_space)
-    ]
-    mine = functools.reduce(jnp.add, [part.astype(jnp.float32) for part in got]).astype(jnp.bfloat16)
-    column = jnp.stack(
-        [mine] + [lax.ppermute(mine, "cons", cons_steps[s]) for s in range(1, n_cons)]
-    )
-    plane = [column] + [
-        lax.ppermute(column, "space", space_steps[s]) for s in range(1, n_space)
-    ]
-    parts = list(plane)
-    for s in range(1, n_spin):
-        parts += [lax.ppermute(part, "spin", spin_steps[s]) for part in plane]
+
+    def over_space(x, s):
+        return lax.ppermute(x, "space", space_steps[s])
+
+    def over_cons(x, s):
+        return lax.ppermute(x, "cons", cons_steps[s])
+
+    got = [sends[0]] + [over_space(sends[s], s) for s in range(1, n_space)]
+    mine = functools.reduce(jnp.add, [part.astype(jnp.float32) for part in got])
+    mine = mine.astype(jnp.bfloat16)
+    pieces = [mine] + [over_cons(mine, s) for s in range(1, n_cons)]
+    own = jnp.stack(pieces).reshape(-1, nev)
+    rows = own.shape[0]
+
+    far = []
+    if n_space == 4:
+        across = n_space - 1
+        first = over_space(mine, across)
+        own, first = lax.optimization_barrier((own, first))
+        rest = [over_cons(first, 1)] + [over_space(pieces[s], across) for s in range(2, n_cons)]
+        place = across * rows
+        far = [(first, place), (jnp.stack(rest).reshape(-1, nev), place + mine.shape[0])]
+    near = range(1, n_space - 1 if far else n_space)
+    held = [(own, 0)] + far + [(over_space(own, s), s * rows) for s in near]
+    for c in range(1, n_spin):
+        held += [
+            (lax.ppermute(part, "spin", spin_steps[c]), c * n_space * rows + place)
+            for part, place in held[: len(far) + len(near) + 1]
+        ]
     layout = (n_space, n_spin, n_cons, nt, nsp, nj)
-    return contract(op_list[0], live_count, elementals, parts, layout)
+    return contract(op_list[0].T, live_count, elementals, *zip(*held), layout)
 
 
 def solution(mesh):

time: 45.3 us -> 40.7 us (0.90)
  the two profiles are of different devices: /device:TPU:0 before, /device:TPU:24 now
where the time goes in v1:
time: 40.7 us; the launch traced here: 40.3 us
  waiting for transfers between devices  14.9 us (37%)
  starting transfers between devices  13.5 us (33%)
  Pallas kernels  11.1 us (27%)
  between operations  0.72 us (2%)
    ppermute x8, waiting for transfers between devices, over_space(): return lax.ppermute(x, 'space', space_steps[s])  12.3 us
    ppermute x8, starting transfers between devices, over_space(): return lax.ppermute(x, 'space', space_steps[s])  7.91 us
    pallas_call x1, Pallas kernels, contract(): pl.pallas_call(functools.partial(contract_kernel, layout, firsts, chunk /...  6.71 us
    ppermute x4, starting transfers between devices, over_cons(): return lax.ppermute(x, 'cons', cons_steps[s])  4.45 us
    pallas_call x1, Pallas kernels, partial_taus(): pl.pallas_call(functools.partial(partial_kernel, n_space, cuts), out_shap...  4.34 us
    ppermute x4, waiting for transfers between devices, over_cons(): return lax.ppermute(x, 'cons', cons_steps[s])  1.94 us
    ppermute x5, starting transfers between devices, body(): lax.ppermute(part, 'spin', spin_steps[c])  1.16 us
  transfers between devices with their start and end apart: 17, of which 9 were waited for; matrix products, arithmetic and copies ran while one was open for 0% of the time, Pallas kernels for 0%

profile of v1, /device:TPU:24, one launch (start us, length us, event | category | flops | bytes accessed | tf_op | source)
XLA Modules:
  0.0 40.3 jit_solution(7184943157343947443)
XLA Ops:
  0.0 0.0 copy-start
  0.0 0.0 copy-start.1
  0.0 4.3 %shard_map.55 = (f32[128,256]{1,0:T(8,128)S(1)}, bf16[128,256]{1,0:T(8,128)(2,1)S(1)}, bf16[128,256]{1,0:T(8,128)(2,1)S(1)}, bf16[128,256]{1,0:T(8,128)(2,1)S(1)}) custom-call(bf16[2,2,256,1920]{3,2,1,0:T(8,128)(2,1)} %v_ref.1, bf16[2,2,2,64,1920]{4,3,2,1,0:T(8,128)(2,1)} %s_ref.1), custom_call_target="tpu_custom_call" | custom-call | flops 1006632960 | bytes 6422528 | tf_op jit(solution)/shard_map/pallas_call | solution.py:94
  4.4 1.6 %collective-permute-start = (bf16[128,256]{1,0:T(8,128)(2,1)S(1)}, bf16[128,256]{1,0:T(8,128)(2,1)S(1)}, u32[]{:S(2)}, u32[]{:S(2)}) collective-permute-start(bf16[128,256]{1,0:T(8,128)(2,1)S(1)} %get-tuple-element.22), channel_id=1, source_target_pairs={{0,8},{8,0},{16,24},{24,16},{1,9},{9,1},{17,25},{25,17},{2,10},{10... | collective-permute-start | bytes 196616 | tf_op jit(solution)/shard_map/ppermute | solution.py:248
  5.9 1.5 %collective-permute-start.1 = (bf16[128,256]{1,0:T(8,128)(2,1)S(1)}, bf16[128,256]{1,0:T(8,128)(2,1)S(1)}, u32[]{:S(2)}, u32[]{:S(2)}) collective-permute-start(bf16[128,256]{1,0:T(8,128)(2,1)S(1)} %get-tuple-element.23), channel_id=1, source_target_pairs={{0,16},{8,24},{16,0},{24,8},{1,17},{9,25},{17,1},{25,9},{2,18},{10... | collective-permute-start | bytes 196616 | tf_op jit(solution)/shard_map/ppermute | solution.py:248
  7.4 0.5 %collective-permute-start.2 = (bf16[128,256]{1,0:T(8,128)(2,1)S(1)}, bf16[128,256]{1,0:T(8,128)(2,1)S(1)}, u32[]{:S(2)}, u32[]{:S(2)}) collective-permute-start(bf16[128,256]{1,0:T(8,128)(2,1)S(1)} %get-tuple-element.24), channel_id=1, source_target_pairs={{0,24},{8,16},{16,8},{24,0},{1,25},{9,17},{17,9},{25,1},{2,26},{10... | collective-permute-start | bytes 196616 | tf_op jit(solution)/shard_map/ppermute | solution.py:248
  7.9 0.8 %collective-permute-done = bf16[128,256]{1,0:T(8,128)(2,1)S(1)} collective-permute-done((bf16[128,256]{1,0:T(8,128)(2,1)S(1)}, bf16[128,256]{1,0:T(8,128)(2,1)S(1)}, u32[]{:S(2)}, u32[]{:S(2)}) %collective-permute-start) | collective-permute-done | bytes 65568 | tf_op jit(solution)/shard_map/ppermute | solution.py:248
  8.7 1.5 %collective-permute-done.1 = bf16[128,256]{1,0:T(8,128)(2,1)S(1)} collective-permute-done((bf16[128,256]{1,0:T(8,128)(2,1)S(1)}, bf16[128,256]{1,0:T(8,128)(2,1)S(1)}, u32[]{:S(2)}, u32[]{:S(2)}) %collective-permute-start.1) | collective-permute-done | bytes 65568 | tf_op jit(solution)/shard_map/ppermute | solution.py:248
  10.2 2.4 %collective-permute-done.2 = bf16[128,256]{1,0:T(8,128)(2,1)S(1)} collective-permute-done((bf16[128,256]{1,0:T(8,128)(2,1)S(1)}, bf16[128,256]{1,0:T(8,128)(2,1)S(1)}, u32[]{:S(2)}, u32[]{:S(2)}) %collective-permute-start.2) | collective-permute-done | bytes 65568 | tf_op jit(solution)/shard_map/ppermute | solution.py:248
  12.7 0.3 collective-permute-start.5
  12.9 1.7 %collective-permute-start.4 = (bf16[128,256]{1,0:T(8,128)(2,1)S(1)}, bf16[128,256]{1,0:T(8,128)(2,1)S(1)}, u32[]{:S(2)}, u32[]{:S(2)}) collective-permute-start(bf16[128,256]{1,0:T(8,128)(2,1)S(1)} %add_convert_fusion), channel_id=1, source_target_pairs={{0,2},{1,3},{2,0},{3,1},{4,6},{5,7},{6,4},{7,5},{8,10},{9,11},{10,... | collective-permute-start | bytes 196616 | tf_op jit(solution)/shard_map/ppermute | solution.py:251
  14.6 2.5 %collective-permute-start.3 = (bf16[128,256]{1,0:T(8,128)(2,1)S(1)}, bf16[128,256]{1,0:T(8,128)(2,1)S(1)}, u32[]{:S(2)}, u32[]{:S(2)}) collective-permute-start(bf16[128,256]{1,0:T(8,128)(2,1)S(1)} %add_convert_fusion), channel_id=1, source_target_pairs={{0,1},{1,0},{2,3},{3,2},{4,5},{5,4},{6,7},{7,6},{8,9},{9,8},{10,11... | collective-permute-start | bytes 196616 | tf_op jit(solution)/shard_map/ppermute | solution.py:251
  17.1 0.5 %collective-permute-start.6 = (bf16[128,256]{1,0:T(8,128)(2,1)S(1)}, bf16[128,256]{1,0:T(8,128)(2,1)S(1)}, u32[]{:S(2)}, u32[]{:S(2)}) collective-permute-start(bf16[128,256]{1,0:T(8,128)(2,1)S(1)} %add_convert_fusion), channel_id=1, source_target_pairs={{0,24},{8,16},{16,8},{24,0},{1,25},{9,17},{17,9},{25,1},{2,26},{10... | collective-permute-start | bytes 196616 | tf_op jit(solution)/shard_map/ppermute | solution.py:248
  17.6 1.3 %collective-permute-done.5 = bf16[128,256]{1,0:T(8,128)(2,1)S(1)} collective-permute-done((bf16[128,256]{1,0:T(8,128)(2,1)S(1)}, bf16[128,256]{1,0:T(8,128)(2,1)S(1)}, u32[]{:S(2)}, u32[]{:S(2)}) %collective-permute-start.5) | collective-permute-done | bytes 65568 | tf_op jit(solution)/shard_map/ppermute | solution.py:251
  18.8 0.0 collective-permute-done.4
  18.8 0.7 %collective-permute-done.3 = bf16[128,256]{1,0:T(8,128)(2,1)S(1)} collective-permute-done((bf16[128,256]{1,0:T(8,128)(2,1)S(1)}, bf16[128,256]{1,0:T(8,128)(2,1)S(1)}, u32[]{:S(2)}, u32[]{:S(2)}) %collective-permute-start.3) | collective-permute-done | bytes 65568 | tf_op jit(solution)/shard_map/ppermute | solution.py:251
  19.5 2.8 %collective-permute-done.6 = bf16[128,256]{1,0:T(8,128)(2,1)S(1)} collective-permute-done((bf16[128,256]{1,0:T(8,128)(2,1)S(1)}, bf16[128,256]{1,0:T(8,128)(2,1)S(1)}, u32[]{:S(2)}, u32[]{:S(2)}) %collective-permute-start.6) | collective-permute-done | bytes 65568 | tf_op jit(solution)/shard_map/ppermute | solution.py:248
  22.4 0.5 %collective-permute-start.11 = (bf16[512,256]{1,0:T(8,128)(2,1)S(1)}, bf16[512,256]{1,0:T(8,128)(2,1)S(1)}, u32[]{:S(2)}, u32[]{:S(2)}) collective-permute-start(bf16[512,256]{1,0:T(8,128)(2,1)S(1)} %bitcast.22), channel_id=1, source_target_pairs={{0,16},{8,24},{16,0},{24,8},{1,17},{9,25},{17,1},{25,9},{2,18},{10... | collective-permute-start | bytes 786440 | tf_op jit(solution)/shard_map/ppermute | solution.py:248
  22.9 0.5 %collective-permute-start.10 = (bf16[512,256]{1,0:T(8,128)(2,1)S(1)}, bf16[512,256]{1,0:T(8,128)(2,1)S(1)}, u32[]{:S(2)}, u32[]{:S(2)}) collective-permute-start(bf16[512,256]{1,0:T(8,128)(2,1)S(1)} %bitcast.23), channel_id=1, source_target_pairs={{0,8},{8,0},{16,24},{24,16},{1,9},{9,1},{17,25},{25,17},{2,10},{10... | collective-permute-start | bytes 786440 | tf_op jit(solution)/shard_map/ppermute | solution.py:248
  23.3 2.5 %collective-permute-start.9 = (bf16[128,256]{1,0:T(8,128)(2,1)S(1)}, bf16[128,256]{1,0:T(8,128)(2,1)S(1)}, u32[]{:S(2)}, u32[]{:S(2)}) collective-permute-start(bf16[128,256]{1,0:T(8,128)(2,1)S(1)} %collective-permute-done.5), channel_id=1, source_target_pairs={{0,24},{8,16},{16,8},{24,0},{1,25},{9,17},{17,9},{25,1},{2,26},{10... | collective-permute-start | bytes 196616 | tf_op jit(solution)/shard_map/ppermute | solution.py:248
  25.9 0.4 %collective-permute-start.8 = (bf16[128,256]{1,0:T(8,128)(2,1)S(1)}, bf16[128,256]{1,0:T(8,128)(2,1)S(1)}, u32[]{:S(2)}, u32[]{:S(2)}) collective-permute-start(bf16[128,256]{1,0:T(8,128)(2,1)S(1)} %collective-permute-done.4), channel_id=1, source_target_pairs={{0,24},{8,16},{16,8},{24,0},{1,25},{9,17},{17,9},{25,1},{2,26},{10... | collective-permute-start | bytes 196616 | tf_op jit(solution)/shard_map/ppermute | solution.py:248
  26.3 0.0 collective-permute-start.7
  26.3 4.6 %collective-permute-done.9 = bf16[128,256]{1,0:T(8,128)(2,1)S(1)} collective-permute-done((bf16[128,256]{1,0:T(8,128)(2,1)S(1)}, bf16[128,256]{1,0:T(8,128)(2,1)S(1)}, u32[]{:S(2)}, u32[]{:S(2)}) %collective-permute-start.9) | collective-permute-done | bytes 65568 | tf_op jit(solution)/shard_map/ppermute | solution.py:248
  30.9 0.0 collective-permute-start.12
  30.9 0.0 collective-permute-done.11
  30.9 0.5 %collective-permute-start.16 = (bf16[512,256]{1,0:T(8,128)(2,1)S(1)}, bf16[512,256]{1,0:T(8,128)(2,1)S(1)}, u32[]{:S(2)}, u32[]{:S(2)}) collective-permute-start(bf16[512,256]{1,0:T(8,128)(2,1)S(1)} %collective-permute-done.11), channel_id=1, source_target_pairs={{0,4},{4,0},{1,5},{5,1},{2,6},{6,2},{3,7},{7,3},{8,12},{12,8},{9,1... | collective-permute-start | bytes 786440 | tf_op jit(solution)/shard_map/ppermute | solution.py:272
  31.4 0.0 collective-permute-done.10
  31.4 0.1 collective-permute-start.15
  31.5 0.1 collective-permute-done.8
  31.6 0.0 collective-permute-done.7
  31.6 0.4 collective-permute-start.14
  32.0 0.2 collective-permute-start.13
  32.9 0.7 %collective-permute-done.13 = bf16[128,256]{1,0:T(8,128)(2,1)S(1)} collective-permute-done((bf16[128,256]{1,0:T(8,128)(2,1)S(1)}, bf16[128,256]{1,0:T(8,128)(2,1)S(1)}, u32[]{:S(2)}, u32[]{:S(2)}) %collective-permute-start.13) | collective-permute-done | bytes 65568 | tf_op jit(solution)/shard_map/ppermute | solution.py:272
  33.6 0.0 collective-permute-done.14
  33.6 0.0 collective-permute-done.12
  33.6 0.0 collective-permute-done.16
  33.6 0.0 collective-permute-done.15
  33.6 0.0 copy-done
  33.6 0.0 copy-done.1
  33.6 6.7 %shard_map.56 = bf16[2,16,256,256]{3,2,1,0:T(8,128)(2,1)} custom-call(s32[4,16]{1,0:T(4,128)S(1)} %bitcast.36, s32[1]{0:T(128)S(6)} %copy.6.live_in, bf16[8,2,256,256]{3,2,1,0:T(8,128)(2,1)S(1)} %copy-done, bf16[8,64,256]{2,1,0:T(8,128)(2,1)S(1)} %bitcast.25, bf16[2,64,256]{2,1,0:T(8,128)(2,1)S(1)} %bitcast.34, bf16[6,64,256]{2,1,0:T(8,128)(2,1)S(1)} %bitcast.27, ...), custom_call_target="tpu_custom_call" | custom-call | flops 4294967296 | bytes 6291456 | tf_op jit(solution)/shard_map/pallas_call | solution.py:211
  (3 shorter events, 0.1 us)
Async XLA Ops:
  0.0 33.6 %copy-start = (bf16[8,2,256,256]{3,2,1,0:T(8,128)(2,1)S(1)}, bf16[8,2,256,256]{3,2,1,0:T(8,128)(2,1)}, u32[]{:S(2)}) copy-start(bf16[8,2,256,256]{3,2,1,0:T(8,128)(2,1)} %elems) | copy-start | bytes 6291460
  0.0 33.6 %copy-start.1 = (s32[1,16,4]{1,2,0:T(4,128)S(1)}, s32[1,16,4]{1,2,0:T(4,128)}, u32[]{:S(2)}) copy-start(s32[1,16,4]{1,2,0:T(4,128)} %param.8) | copy-start | bytes 772
  4.4 4.3 %collective-permute-start = (bf16[128,256]{1,0:T(8,128)(2,1)S(1)}, bf16[128,256]{1,0:T(8,128)(2,1)S(1)}, u32[]{:S(2)}, u32[]{:S(2)}) collective-permute-start(bf16[128,256]{1,0:T(8,128)(2,1)S(1)} %get-tuple-element.22), channel_id=1, source_target_pairs={{0,8},{8,0},{16,24},{24,16},{1,9},{9,1},{17,25},{25,17},{2,10},{10... | collective-permute-start | bytes 196616 | tf_op jit(solution)/shard_map/ppermute | solution.py:248
  5.9 4.3 %collective-permute-start.1 = (bf16[128,256]{1,0:T(8,128)(2,1)S(1)}, bf16[128,256]{1,0:T(8,128)(2,1)S(1)}, u32[]{:S(2)}, u32[]{:S(2)}) collective-permute-start(bf16[128,256]{1,0:T(8,128)(2,1)S(1)} %get-tuple-element.23), channel_id=1, source_target_pairs={{0,16},{8,24},{16,0},{24,8},{1,17},{9,25},{17,1},{25,9},{2,18},{10... | collective-permute-start | bytes 196616 | tf_op jit(solution)/shard_map/ppermute | solution.py:248
  7.4 5.2 %collective-permute-start.2 = (bf16[128,256]{1,0:T(8,128)(2,1)S(1)}, bf16[128,256]{1,0:T(8,128)(2,1)S(1)}, u32[]{:S(2)}, u32[]{:S(2)}) collective-permute-start(bf16[128,256]{1,0:T(8,128)(2,1)S(1)} %get-tuple-element.24), channel_id=1, source_target_pairs={{0,24},{8,16},{16,8},{24,0},{1,25},{9,17},{17,9},{25,1},{2,26},{10... | collective-permute-start | bytes 196616 | tf_op jit(solution)/shard_map/ppermute | solution.py:248
  12.7 6.2 %collective-permute-start.5 = (bf16[128,256]{1,0:T(8,128)(2,1)S(1)}, bf16[128,256]{1,0:T(8,128)(2,1)S(1)}, u32[]{:S(2)}, u32[]{:S(2)}) collective-permute-start(bf16[128,256]{1,0:T(8,128)(2,1)S(1)} %add_convert_fusion), channel_id=1, source_target_pairs={{0,3},{1,2},{2,1},{3,0},{4,7},{5,6},{6,5},{7,4},{8,11},{9,10},{10,... | collective-permute-start | bytes 196616 | tf_op jit(solution)/shard_map/ppermute | solution.py:251
  12.9 5.9 %collective-permute-start.4 = (bf16[128,256]{1,0:T(8,128)(2,1)S(1)}, bf16[128,256]{1,0:T(8,128)(2,1)S(1)}, u32[]{:S(2)}, u32[]{:S(2)}) collective-permute-start(bf16[128,256]{1,0:T(8,128)(2,1)S(1)} %add_convert_fusion), channel_id=1, source_target_pairs={{0,2},{1,3},{2,0},{3,1},{4,6},{5,7},{6,4},{7,5},{8,10},{9,11},{10,... | collective-permute-start | bytes 196616 | tf_op jit(solution)/shard_map/ppermute | solution.py:251
  14.6 4.9 %collective-permute-start.3 = (bf16[128,256]{1,0:T(8,128)(2,1)S(1)}, bf16[128,256]{1,0:T(8,128)(2,1)S(1)}, u32[]{:S(2)}, u32[]{:S(2)}) collective-permute-start(bf16[128,256]{1,0:T(8,128)(2,1)S(1)} %add_convert_fusion), channel_id=1, source_target_pairs={{0,1},{1,0},{2,3},{3,2},{4,5},{5,4},{6,7},{7,6},{8,9},{9,8},{10,11... | collective-permute-start | bytes 196616 | tf_op jit(solution)/shard_map/ppermute | solution.py:251
  17.1 5.3 %collective-permute-start.6 = (bf16[128,256]{1,0:T(8,128)(2,1)S(1)}, bf16[128,256]{1,0:T(8,128)(2,1)S(1)}, u32[]{:S(2)}, u32[]{:S(2)}) collective-permute-start(bf16[128,256]{1,0:T(8,128)(2,1)S(1)} %add_convert_fusion), channel_id=1, source_target_pairs={{0,24},{8,16},{16,8},{24,0},{1,25},{9,17},{17,9},{25,1},{2,26},{10... | collective-permute-start | bytes 196616 | tf_op jit(solution)/shard_map/ppermute | solution.py:248
  22.4 8.5 %collective-permute-start.11 = (bf16[512,256]{1,0:T(8,128)(2,1)S(1)}, bf16[512,256]{1,0:T(8,128)(2,1)S(1)}, u32[]{:S(2)}, u32[]{:S(2)}) collective-permute-start(bf16[512,256]{1,0:T(8,128)(2,1)S(1)} %bitcast.22), channel_id=1, source_target_pairs={{0,16},{8,24},{16,0},{24,8},{1,17},{9,25},{17,1},{25,9},{2,18},{10... | collective-permute-start | bytes 786440 | tf_op jit(solution)/shard_map/ppermute | solution.py:248
  22.9 8.6 %collective-permute-start.10 = (bf16[512,256]{1,0:T(8,128)(2,1)S(1)}, bf16[512,256]{1,0:T(8,128)(2,1)S(1)}, u32[]{:S(2)}, u32[]{:S(2)}) collective-permute-start(bf16[512,256]{1,0:T(8,128)(2,1)S(1)} %bitcast.23), channel_id=1, source_target_pairs={{0,8},{8,0},{16,24},{24,16},{1,9},{9,1},{17,25},{25,17},{2,10},{10... | collective-permute-start | bytes 786440 | tf_op jit(solution)/shard_map/ppermute | solution.py:248
  23.3 7.6 %collective-permute-start.9 = (bf16[128,256]{1,0:T(8,128)(2,1)S(1)}, bf16[128,256]{1,0:T(8,128)(2,1)S(1)}, u32[]{:S(2)}, u32[]{:S(2)}) collective-permute-start(bf16[128,256]{1,0:T(8,128)(2,1)S(1)} %collective-permute-done.5), channel_id=1, source_target_pairs={{0,24},{8,16},{16,8},{24,0},{1,25},{9,17},{17,9},{25,1},{2,26},{10... | collective-permute-start | bytes 196616 | tf_op jit(solution)/shard_map/ppermute | solution.py:248
  25.9 5.8 %collective-permute-start.8 = (bf16[128,256]{1,0:T(8,128)(2,1)S(1)}, bf16[128,256]{1,0:T(8,128)(2,1)S(1)}, u32[]{:S(2)}, u32[]{:S(2)}) collective-permute-start(bf16[128,256]{1,0:T(8,128)(2,1)S(1)} %collective-permute-done.4), channel_id=1, source_target_pairs={{0,24},{8,16},{16,8},{24,0},{1,25},{9,17},{17,9},{25,1},{2,26},{10... | collective-permute-start | bytes 196616 | tf_op jit(solution)/shard_map/ppermute | solution.py:248
  26.3 5.3 %collective-permute-start.7 = (bf16[128,256]{1,0:T(8,128)(2,1)S(1)}, bf16[128,256]{1,0:T(8,128)(2,1)S(1)}, u32[]{:S(2)}, u32[]{:S(2)}) collective-permute-start(bf16[128,256]{1,0:T(8,128)(2,1)S(1)} %collective-permute-done.6), channel_id=1, source_target_pairs={{0,1},{1,0},{2,3},{3,2},{4,5},{5,4},{6,7},{7,6},{8,9},{9,8},{10,11... | collective-permute-start | bytes 196616 | tf_op jit(solution)/shard_map/ppermute | solution.py:251
  30.9 2.7 %collective-permute-start.12 = (bf16[512,256]{1,0:T(8,128)(2,1)S(1)}, bf16[512,256]{1,0:T(8,128)(2,1)S(1)}, u32[]{:S(2)}, u32[]{:S(2)}) collective-permute-start(bf16[512,256]{1,0:T(8,128)(2,1)S(1)} %bitcast.24), channel_id=1, source_target_pairs={{0,4},{4,0},{1,5},{5,1},{2,6},{6,2},{3,7},{7,3},{8,12},{12,8},{9,1... | collective-permute-start | bytes 786440 | tf_op jit(solution)/shard_map/ppermute | solution.py:272
  30.9 2.7 %collective-permute-start.16 = (bf16[512,256]{1,0:T(8,128)(2,1)S(1)}, bf16[512,256]{1,0:T(8,128)(2,1)S(1)}, u32[]{:S(2)}, u32[]{:S(2)}) collective-permute-start(bf16[512,256]{1,0:T(8,128)(2,1)S(1)} %collective-permute-done.11), channel_id=1, source_target_pairs={{0,4},{4,0},{1,5},{5,1},{2,6},{6,2},{3,7},{7,3},{8,12},{12,8},{9,1... | collective-permute-start | bytes 786440 | tf_op jit(solution)/shard_map/ppermute | solution.py:272
  31.4 2.2 %collective-permute-start.15 = (bf16[512,256]{1,0:T(8,128)(2,1)S(1)}, bf16[512,256]{1,0:T(8,128)(2,1)S(1)}, u32[]{:S(2)}, u32[]{:S(2)}) collective-permute-start(bf16[512,256]{1,0:T(8,128)(2,1)S(1)} %collective-permute-done.10), channel_id=1, source_target_pairs={{0,4},{4,0},{1,5},{5,1},{2,6},{6,2},{3,7},{7,3},{8,12},{12,8},{9,1... | collective-permute-start | bytes 786440 | tf_op jit(solution)/shard_map/ppermute | solution.py:272
  31.6 1.9 %collective-permute-start.14 = (bf16[384,256]{1,0:T(8,128)(2,1)S(1)}, bf16[384,256]{1,0:T(8,128)(2,1)S(1)}, u32[]{:S(2)}, u32[]{:S(2)}) collective-permute-start(bf16[384,256]{1,0:T(8,128)(2,1)S(1)} %bitcast.26), channel_id=1, source_target_pairs={{0,4},{4,0},{1,5},{5,1},{2,6},{6,2},{3,7},{7,3},{8,12},{12,8},{9,1... | collective-permute-start | bytes 589832 | tf_op jit(solution)/shard_map/ppermute | solution.py:272
  32.0 1.5 %collective-permute-start.13 = (bf16[128,256]{1,0:T(8,128)(2,1)S(1)}, bf16[128,256]{1,0:T(8,128)(2,1)S(1)}, u32[]{:S(2)}, u32[]{:S(2)}) collective-permute-start(bf16[128,256]{1,0:T(8,128)(2,1)S(1)} %collective-permute-done.6), channel_id=1, source_target_pairs={{0,4},{4,0},{1,5},{5,1},{2,6},{6,2},{3,7},{7,3},{8,12},{12,8},{9,1... | collective-permute-start | bytes 196616 | tf_op jit(solution)/shard_map/ppermute | solution.py:272
